TPU v7x, 32 devices: a whole 2x2x4 slice. The times are simulated.
32 devices in a mesh: seq: 8 (over z, x), head: 4 (over y, core).
Axes of the slice: x: 2, y: 2, z: 4, core: 2. Of those that a mesh axis runs over, the one named last changes fastest.
Arguments:
- queries: bfloat16 [2, 2048, 2048], P(None, 'seq', 'head'), may hold values from -1.75 to 1.75
- keys: bfloat16 [2, 2048, 2048], P(None, 'seq', 'head'), may hold values from -1.75 to 1.75
- values: bfloat16 [2, 2048, 2048], P(None, 'seq', 'head'), may hold values from -6 to 6
- gate_pre: bfloat16 [2, 2048, 2048], P(None, 'seq', 'head'), may hold values from -8 to 8
- grad_out: bfloat16 [2, 2048, 4096], P(None, 'seq', 'head'), may hold values from -6 to 6
- w_query: bfloat16 [4096, 2048], P(None, 'head'), may hold values from -0.09375 to 0.09375
- w_key: bfloat16 [4096, 2048], P(None, 'head'), may hold values from -0.09375 to 0.09375
- w_value: bfloat16 [4096, 2048], P(None, 'head'), may hold values from -0.09375 to 0.09375
- w_gate: bfloat16 [4096, 2048], P(None, 'head'), may hold values from -0.09375 to 0.09375
- w_out: bfloat16 [2048, 4096], P('head'), may hold values from -0.125 to 0.125
Outputs:
- grad_in: bfloat16 [2, 2048, 4096], P(None, 'seq', 'head')
All inputs are finite; a program needn't handle non-finite values.
Results may differ from a plain program's by a relative error of at most 0.022.
Values may be sent and summed in bfloat16 or wider, within the bound.
A program may use at most 128 MiB of HBM per device.

v0:
```python
import jax
import jax.numpy as jnp
from jax import lax
from jax.sharding import PartitionSpec as P

HD = 128


def entering(x, axis, combine, identity, reverse):
    peers, here = (lax.axis_size(axis), lax.axis_index(axis))
    everything = lax.all_gather(x.astype(jnp.bfloat16), axis)
    start = jnp.broadcast_to(jnp.asarray(identity, x.dtype), x.shape)

    def step(k, before):
        at = peers - 1 - k if reverse else k
        reached = at > here if reverse else at < here
        new = combine(before, everything[at].astype(x.dtype))
        return jnp.where(reached, new, before)

    return lax.fori_loop(0, peers, step, start)


def add_states(earlier, later):
    return earlier + later


def body(queries, keys, values, gate_pre, grad_out, w_query, w_key, w_value, w_gate, w_out):
    seq_count, block_len, columns = queries.shape
    head_count = columns // HD
    factor = (lax.axis_size("seq") * block_len) ** (-0.5)
    exact = lax.Precision.HIGHEST
    d_gated = jnp.einsum(
        "scd,jd->scj",
        lax.all_gather(grad_out, "head", axis=2, tiled=True),
        w_out,
        preferred_element_type=jnp.float32,
    )
    gate_open = jax.nn.sigmoid(gate_pre.astype(jnp.float32))
    d_output = (d_gated * gate_open).astype(jnp.bfloat16)

    def split_heads(tensor):
        return tensor.reshape(seq_count, block_len, head_count, HD)

    query_heads = split_heads(queries)
    key_heads = split_heads(keys)
    value_heads = split_heads(values)
    grad_heads = split_heads(d_output)
    key_state = jnp.einsum(
        "schk,schv->shkv", key_heads, value_heads, preferred_element_type=jnp.float32
    )
    query_state = jnp.einsum(
        "schk,schv->shkv", query_heads, grad_heads, preferred_element_type=jnp.float32
    )
    prefix = entering(key_state, "seq", add_states, jnp.zeros_like(key_state), False)
    suffix = entering(query_state, "seq", add_states, jnp.zeros_like(query_state), True)
    causal = jnp.tril(jnp.ones((block_len, block_len), dtype=bool))
    scores = jnp.where(
        causal,
        jnp.einsum("sthk,suhk->shtu", query_heads, key_heads, preferred_element_type=jnp.float32),
        0.0,
    ).astype(jnp.bfloat16)
    backward = jnp.where(
        causal,
        jnp.einsum("sthv,suhv->shtu", grad_heads, value_heads, preferred_element_type=jnp.float32),
        0.0,
    ).astype(jnp.bfloat16)
    attended = factor * (
        jnp.einsum("sthk,shkv->sthv", query_heads.astype(jnp.float32), prefix, precision=exact)
        + jnp.einsum("shtu,suhv->sthv", scores, value_heads, preferred_element_type=jnp.float32)
    )
    d_gate = (
        d_gated * attended.reshape(seq_count, block_len, columns) * gate_open * (1.0 - gate_open)
    ).astype(jnp.bfloat16)
    d_query = factor * (
        jnp.einsum("sthv,shkv->sthk", grad_heads.astype(jnp.float32), prefix, precision=exact)
        + jnp.einsum("shtu,suhk->sthk", backward, key_heads, preferred_element_type=jnp.float32)
    )
    d_key = factor * (
        jnp.einsum("shtu,sthk->suhk", backward, query_heads, preferred_element_type=jnp.float32)
        + jnp.einsum("suhv,shkv->suhk", value_heads.astype(jnp.float32), suffix, precision=exact)
    )
    d_value = factor * (
        jnp.einsum("shtu,sthv->suhv", scores, grad_heads, preferred_element_type=jnp.float32)
        + jnp.einsum("suhk,shkv->suhv", key_heads.astype(jnp.float32), suffix, precision=exact)
    )
    d_query = d_query.astype(jnp.bfloat16).reshape(seq_count, block_len, columns)
    d_key = d_key.astype(jnp.bfloat16).reshape(seq_count, block_len, columns)
    d_value = d_value.astype(jnp.bfloat16).reshape(seq_count, block_len, columns)
    partial_sum = jnp.einsum("scj,dj->scd", d_query, w_query, preferred_element_type=jnp.float32)
    partial_sum = partial_sum + jnp.einsum(
        "scj,dj->scd", d_key, w_key, preferred_element_type=jnp.float32
    )
    partial_sum = partial_sum + jnp.einsum(
        "scj,dj->scd", d_value, w_value, preferred_element_type=jnp.float32
    )
    partial_sum = partial_sum + jnp.einsum(
        "scj,dj->scd", d_gate, w_gate, preferred_element_type=jnp.float32
    )
    return lax.psum_scatter(
        partial_sum.astype(jnp.bfloat16), "head", scatter_dimension=2, tiled=True
    )


def solution(mesh):
    return jax.shard_map(
        body,
        mesh=mesh,
        in_specs=(
            P(None, "seq", "head"),
            P(None, "seq", "head"),
            P(None, "seq", "head"),
            P(None, "seq", "head"),
            P(None, "seq", "head"),
            P(None, "head"),
            P(None, "head"),
            P(None, "head"),
            P(None, "head"),
            P("head", None),
        ),
        out_specs=P(None, "seq", "head"),
        check_vma=False,
    )
```

profile of v0, /device:TPU:0, one launch (start us, length us, event | category | flops | bytes accessed | tf_op | source)
XLA Modules:
  0.0 234.5 jit_solution(138246326557114444)
XLA Ops:
  7.3 1.3 copy.63
  8.6 2.1 convolution_convert_fusion.1
  10.9 1.5 select_convert_fusion
  13.3 1.5 convolution_bitcast_fusion.4
  14.8 31.3 %all-gather.6.cloned.1.call-done = bf16[2,256,4096]{2,1,0:T(8,128)(2,1)} async-done(((bf16[2,256,1024]{2,1,0:T(8,128)(2,1)}), bf16[2,256,4096]{2,1,0:T(8,128)(2,1)}) %all-gather.6.cloned.1.call-update) | async-done | bytes 4194320 | tf_op jit(solution)/shard_map/all_gather | solution.py:34
  46.1 6.8 %multiply_convert_fusion.1 = (bf16[2,256,512]{2,1,0:T(8,128)(2,1)S(1)}, f32[2,256,512]{2,1,0:T(8,128)}) fusion(bf16[2,256,512]{2,1,0:T(8,128)(2,1)S(1)} %copy-done.10, bf16[2,256,4096]{2,1,0:T(8,128)(2,1)} %all-gather.6.cloned.1.call-done, bf16[512,4096]{1,0:T(8,128)(2,1)} %param.23), kind=kOutput, calls=%fused_computation.35 | convolution fusion | flops 2149056512 | bytes 10485760 | tf_op jit(solution)/shard_map/scd,jd->scj/dot_general | solution.py:32
  54.5 43.0 %all-gather.8.cloned.1.call-done = bf16[16,4,128,128]{3,2,1,0:T(8,128)(2,1)} async-done(((bf16[2,4,128,128]{3,2,1,0:T(8,128)(2,1)}), bf16[16,4,128,128]{3,2,1,0:T(8,128)(2,1)}) %all-gather.8.cloned.1.call-update) | async-done | bytes 2097168 | tf_op jit(solution)/shard_map/all_gather | solution.py:11
  97.6 10.1 %while.30 = (s32[]{:T(128)}, f32[2,4,128,128]{3,2,1,0:T(8,128)S(1)}, s32[]{:T(128)}, bf16[8,2,4,128,128]{4,3,2,1,0:T(8,128)(2,1)}, s32[]{:T(128)}, /*index=5*/s32[]{:T(128)}) while((s32[]{:T(128)}, f32[2,4,128,128]{3,2,1,0:T(8,128)S(1)}, s32[]{:T(128)}, bf16[8,2,4,128,128]{4,3,2,1,0:T(8,128)(2,1)}, s32[]{:T(128)}, ...), condition=%wide.region_1.2_spmd.clone, body=%wide.region_0.1_spmd.clone.sunk | while | flops 524292 | bytes 1310821 | solution.py:20
  98.8 1.2 add_select_fusion.4
  105.1 1.2 add_select_fusion.4
  106.4 1.3 add_select_fusion.4
  107.7 2.9 %fusion.10 = f32[2,256,4,128]{1,3,2,0:T(8,128)} fusion(f32[2,256,4,128]{1,3,2,0:T(8,128)} %convolution_bitcast_fusion.4, f32[2,4,128,128]{3,2,1,0:T(8,128)S(1)} %get-tuple-element.194, bf16[2,256,512]{2,1,0:T(8,128)(2,1)S(1)} %copy-done), kind=kOutput, calls=%fused_computation.16 | convolution fusion | flops 403177472 | bytes 3145728 | tf_op jit(solution)/shard_map/sthk,shkv->sthv/dot_general | solution.py:68
  110.6 2.6 %copy.62 = f32[2,256,512]{2,1,0:T(8,128)} copy(f32[2,256,512]{1,2,0:T(8,128)} %bitcast.139) | data formatting | bytes 2097152 | tf_op jit(solution)/shard_map/reshape | solution.py:72
  113.7 2.5 %fusion.38 = f32[2,4,128,256]{3,2,1,0:T(8,128)} fusion(bf16[2,256,4,128]{1,3,2,0:T(8,128)(2,1)S(1)} %bitcast.137, bf16[2,4,256,256]{3,2,1,0:T(8,128)(2,1)} %copy-done.7), kind=kOutput, calls=%fused_computation.56 | convolution fusion | flops 134217728 | bytes 2621440 | tf_op jit(solution)/shard_map/shtu,sthv->suhv/dot_general | solution.py:83
  116.2 1.4 convolution_bitcast_fusion.3
  118.8 5.7 %fusion.5 = f32[2,256,4096]{2,1,0:T(8,128)} fusion(bf16[2,256,512]{1,2,0:T(8,128)(2,1)S(1)} %bitcast.141, bf16[4096,512]{1,0:T(8,128)(2,1)S(1)} %copy-done.3), kind=kOutput, calls=%fused_computation.8 | convolution fusion | flops 2147483648 | bytes 13107200 | tf_op jit(solution)/shard_map/scj,dj->scd/dot_general | solution.py:89
  124.4 23.2 %all-gather.10.cloned.1.call-done = bf16[16,4,128,128]{3,2,1,0:T(8,128)(2,1)} async-done(((bf16[2,4,128,128]{3,2,1,0:T(8,128)(2,1)}), bf16[16,4,128,128]{3,2,1,0:T(8,128)(2,1)}) %all-gather.10.cloned.1.call-update) | async-done | bytes 2097168 | tf_op jit(solution)/shard_map/all_gather | solution.py:11
  147.7 10.2 %while.31 = (s32[]{:T(128)}, f32[2,4,128,128]{3,2,1,0:T(8,128)S(1)}, s32[]{:T(128)}, bf16[8,2,4,128,128]{4,3,2,1,0:T(8,128)(2,1)}, s32[]{:T(128)}, /*index=5*/s32[]{:T(128)}, s32[]{:T(128)}, s32[]{:T(128)}) while((s32[]{:T(128)}, f32[2,4,128,128]{3,2,1,0:T(8,128)S(1)}, s32[]{:T(128)}, bf16[8,2,4,128,128]{4,3,2,1,0:T(8,128)(2,1)}, ...), condition=%wide.region_3.4_spmd.clone, body=%wide.region_2.3_spmd.clone.sunk | while | flops 524296 | bytes 1310883 | solution.py:20
  147.7 1.3 add_select_fusion.5
  157.9 2.0 fusion.18
  160.5 5.7 %fusion.3 = f32[2,256,4096]{2,1,0:T(8,128)} fusion(bf16[2,256,512]{1,2,0:T(8,128)(2,1)S(1)} %bitcast.142, bf16[4096,512]{1,0:T(8,128)(2,1)S(1)} %copy-done.4), kind=kOutput, calls=%fused_computation.6 | convolution fusion | flops 2147483648 | bytes 13107200 | tf_op jit(solution)/shard_map/scj,dj->scd/dot_general | solution.py:90
  166.2 5.6 %fusion.1 = f32[2,256,4096]{2,1,0:T(8,128)} fusion(bf16[2,256,512]{1,2,0:T(8,128)(2,1)S(1)} %bitcast.140, bf16[4096,512]{1,0:T(8,128)(2,1)S(1)} %copy-done.5), kind=kOutput, calls=%fused_computation.4 | convolution fusion | flops 2147483648 | bytes 13107200 | tf_op jit(solution)/shard_map/scj,dj->scd/dot_general | solution.py:93
  171.8 13.0 %add_convert_fusion = bf16[2,256,4096]{2,1,0:T(8,128)(2,1)} fusion(f32[2,256,4096]{2,1,0:T(8,128)} %fusion.1, f32[2,256,4096]{2,1,0:T(8,128)} %fusion.5, f32[2,256,4096]{2,1,0:T(8,128)} %fusion.3, bf16[4096,512]{1,0:T(8,128)(2,1)} %param.22, f32[2,256,512]{2,1,0:T(8,128)S(1)} %copy-done.9, f32[2,256,512]{2,1,0:T(8,128)S(1)} %copy-done.6, ...), kind=kOutput, calls=%fused_computation.2 | convolution fusion | flops 2158231552 | bytes 36175872 | tf_op jit(solution)/shard_map/scj,dj->scd/dot_general | solution.py:96
  184.8 43.1 %reduce-scatter.2.cloned.1.call-done = bf16[2,256,1024]{2,1,0:T(8,128)(2,1)} async-done(((bf16[2,256,4096]{2,1,0:T(8,128)(2,1)}), bf16[2,256,1024]{2,1,0:T(8,128)(2,1)}) %reduce-scatter.2.cloned.1.call-update) | async-done | bytes 1048592 | tf_op jit(solution)/shard_map/reduce_scatter | solution.py:99
  (54 shorter events, 20.6 us)
Async XLA Ops:
  6.5 4.3 %copy-start = (bf16[2,256,512]{2,1,0:T(8,128)(2,1)S(1)}, bf16[2,256,512]{2,1,0:T(8,128)(2,1)}, u32[]{:S(2)}) copy-start(bf16[2,256,512]{2,1,0:T(8,128)(2,1)} %param.14) | copy-start | bytes 1572868
  6.5 39.6 %all-gather.6.cloned.1.call-start = ((), (), s32[]{:S(2)}) async-start(), calls=%async_computation.1 | async-start | bytes 5242880 | tf_op jit(solution)/shard_map/all_gather | solution.py:34
  7.3 38.9 %copy-start.10 = (bf16[2,256,512]{2,1,0:T(8,128)(2,1)S(1)}, bf16[2,256,512]{2,1,0:T(8,128)(2,1)}, u32[]{:S(2)}) copy-start(bf16[2,256,512]{2,1,0:T(8,128)(2,1)} %param.17) | copy-start | bytes 1572868
  7.3 90.3 %all-gather.8.cloned.1.call-start = ((), (), s32[]{:S(2)}) async-start(), calls=%async_computation.3 | async-start | bytes 2359296 | tf_op jit(solution)/shard_map/all_gather | solution.py:11
  10.7 137.0 %all-gather.10.cloned.1.call-start = ((), (), s32[]{:S(2)}) async-start(), calls=%async_computation.4 | async-start | bytes 2359296 | tf_op jit(solution)/shard_map/all_gather | solution.py:11
  12.3 1.0 copy-start.7
  54.3 173.6 %reduce-scatter.2.cloned.1.call-start = ((), (), s32[]{:S(2)}) async-start(), calls=%async_computation.2 | async-start | bytes 5242880 | tf_op jit(solution)/shard_map/reduce_scatter | solution.py:99
  113.2 4.4 %copy-start.2 = (bf16[2,256,512]{2,1,0:T(8,128)(2,1)S(1)}, bf16[2,256,512]{2,1,0:T(8,128)(2,1)}, u32[]{:S(2)}) copy-start(bf16[2,256,512]{2,1,0:T(8,128)(2,1)} %param.15) | copy-start | bytes 1572868
  116.2 2.6 %copy-start.3 = (bf16[4096,512]{1,0:T(8,128)(2,1)S(1)}, bf16[4096,512]{1,0:T(8,128)(2,1)}, u32[]{:S(2)}) copy-start(bf16[4096,512]{1,0:T(8,128)(2,1)} %param.19) | copy-start | bytes 12582916
  147.7 12.2 %copy-start.8 = (f32[2,256,4,128]{1,3,2,0:T(8,128)S(1)}, f32[2,256,4,128]{1,3,2,0:T(8,128)}, u32[]{:S(2)}) copy-start(f32[2,256,4,128]{1,3,2,0:T(8,128)} %convolution_bitcast_fusion.3) | copy-start | bytes 3145732
  157.9 2.6 %copy-start.4 = (bf16[4096,512]{1,0:T(8,128)(2,1)S(1)}, bf16[4096,512]{1,0:T(8,128)(2,1)}, u32[]{:S(2)}) copy-start(bf16[4096,512]{1,0:T(8,128)(2,1)} %param.20) | copy-start | bytes 12582916
  160.5 5.7 %copy-start.5 = (bf16[4096,512]{1,0:T(8,128)(2,1)S(1)}, bf16[4096,512]{1,0:T(8,128)(2,1)}, u32[]{:S(2)}) copy-start(bf16[4096,512]{1,0:T(8,128)(2,1)} %param.21) | copy-start | bytes 12582916
  166.2 5.6 %copy-start.6 = (f32[2,256,512]{2,1,0:T(8,128)S(1)}, f32[2,256,512]{2,1,0:T(8,128)}, u32[]{:S(2)}) copy-start(f32[2,256,512]{2,1,0:T(8,128)} %copy.62) | copy-start | bytes 3145732
  166.2 5.6 %copy-start.9 = (f32[2,256,512]{2,1,0:T(8,128)S(1)}, f32[2,256,512]{2,1,0:T(8,128)}, u32[]{:S(2)}) copy-start(f32[2,256,512]{2,1,0:T(8,128)} %get-tuple-element.247) | copy-start | bytes 3145732
  166.2 5.6 %copy-start.11 = (bf16[2,256,512]{2,1,0:T(8,128)(2,1)S(1)}, bf16[2,256,512]{2,1,0:T(8,128)(2,1)}, u32[]{:S(2)}) copy-start(bf16[2,256,512]{2,1,0:T(8,128)(2,1)} %param.17) | copy-start | bytes 1572868
  171.8 56.2 %copy-start.1 = (bf16[2,256,512]{2,1,0:T(8,128)(2,1)S(1)}, bf16[2,256,512]{2,1,0:T(8,128)(2,1)}, u32[]{:S(2)}) copy-start(bf16[2,256,512]{2,1,0:T(8,128)(2,1)} %param.14) | copy-start | bytes 1572868
Sparse Core Ops, SparseCore 0:
  8.9 37.1 all-gather.5
  48.3 49.2 all-gather.7
  99.7 47.9 all-gather.9
  184.9 42.9 reduce-scatter.1
where the time goes:
time: 235 us; the launch traced here: 234 us
  waiting for transfers between devices  141 us (60%)
  matrix products  53.1 us (23%)
  other arithmetic  19.9 us (8%)
  between operations  13.3 us (6%)
  local copies, waits for them, and re-layouts  6.08 us (3%)
    all_gather x2, waiting for transfers between devices, entering(): everything = lax.all_gather(x.astype(jnp.bfloat16), axis)  66.3 us
    reduce_scatter x1, waiting for transfers between devices, body(): lax.psum_scatter(partial_sum.astype(jnp.bfloat16), 'head', scatter_dimens...  43.1 us
    all_gather x1, waiting for transfers between devices, body(): lax.all_gather(grad_out, 'head', axis=2, tiled=True)  31.3 us
    select_n x16, other arithmetic, step(): return jnp.where(reached, new, before)  19.9 us
    dot_general x1, matrix products, body(): jnp.einsum('scj,dj->scd', d_gate, w_gate, preferred_element_type=jnp.floa...  13 us
    dot_general x1, matrix products, body(): jnp.einsum('scd,jd->scj', lax.all_gather(grad_out, 'head', axis=2, tiled=...  6.8 us
    dot_general x1, matrix products, body(): jnp.einsum('scj,dj->scd', d_key, w_key, preferred_element_type=jnp.float32)  5.65 us
    dot_general x1, matrix products, body(): jnp.einsum('scj,dj->scd', d_query, w_query, preferred_element_type=jnp.fl...  5.65 us
  transfers between devices with their start and end apart: 4, of which 4 were waited for; matrix products, arithmetic and copies ran while one was open for 18% of the time, Pallas kernels for 0%

commit v1 on v0

v1 whole, which is shorter than its diff:
```python
import functools

import jax
import jax.numpy as jnp
from jax import lax
from jax.experimental import pallas as pl
from jax.experimental.pallas import tpu as pltpu
from jax.sharding import PartitionSpec as P

HD = 128
TILE = 256
MESH = pl.DeviceIdType.MESH
BF16, F32 = jnp.bfloat16, jnp.float32


def dot(a, b, ca, cb):
    return lax.dot_general(a, b, (((ca,), (cb,)), ((), ())), preferred_element_type=F32)


def kernel(
    n, ns,
    q_h, k_h, v_h, g_h, go_h, wq_h, wk_h, wv_h, wg_h, wo_h, out_ref,
    q_v, k_v, v_v, g_v, wo_v, w_v, gbuf, sc, att, dgated, dout, dcat, dki, dvi, acc,
    ks_send, ks_pair, ks_sum, ks_slots, qs_send, qs_pair, qs_sum, qs_slots, state,
    part_send, part_recv, y_send, y_recv, own,
    ld, ld_own, ag_s, ag_f, ag_r, kp, kg_s, kg_r, qp, qg_s, qg_r, ps, pr, ys, yr,
):
    seqs, span, cols = q_v.shape
    feat = go_h.shape[2]
    width = wq_h.shape[0]
    heads = cols // HD
    chips, groups = n // 2, ns // 2
    factor = float(ns * span) ** (-0.5)
    i, j = lax.axis_index("seq"), lax.axis_index("head")
    c, p = j // 2, lax.rem(j, 2)
    g, r = i // 2, lax.rem(i, 2)
    pj, pi = j + 1 - 2 * p, i + 1 - 2 * r
    others = [lax.rem(c + d, chips) for d in range(1, chips)]

    def rc(src, dst, ss, rs, dev):
        return pltpu.make_async_remote_copy(
            src_ref=src, dst_ref=dst, send_sem=ss, recv_sem=rs, device_id=dev, device_id_type=MESH
        )

    barrier = pltpu.get_barrier_semaphore()
    peers = [(i, pj), (pi, j)]
    peers += [(i, 2 * o + p) for o in others]
    peers += [(2 * lax.rem(g + d, groups) + r, j) for d in range(1, groups)]
    for peer in peers:
        pl.semaphore_signal(barrier, inc=1, device_id=peer, device_id_type=MESH)

    pairs = [(k_h, k_v), (v_h, v_v), (q_h, q_v), (wo_h, wo_v), (g_h, g_v)]
    pairs += [(w, w_v.at[x]) for x, w in enumerate((wq_h, wg_h, wk_h, wv_h))]
    loads = [pltpu.make_async_copy(a, b, ld.at[x]) for x, (a, b) in enumerate(pairs)]
    own_loads = [pltpu.make_async_copy(go_h.at[s], gbuf.at[s, j], ld_own.at[s]) for s in range(seqs)]
    for load in loads[:4] + own_loads + loads[4:]:
        load.start()
    pl.semaphore_wait(barrier, len(peers))

    def ag_far(s):
        return [
            rc(go_h.at[s], gbuf.at[s, j], ag_s.at[s, x], ag_r.at[s, j], (i, 2 * o + p))
            for x, o in enumerate(others)
        ]

    def ag_near(s):
        return rc(go_h.at[s], gbuf.at[s, j], ag_s.at[s, chips - 1], ag_r.at[s, j], (i, pj))

    def ag_wait(s, src):
        rc(go_h.at[s], gbuf.at[s, src], ag_s.at[s, 0], ag_r.at[s, src], (i, pj)).wait_recv()

    far = [ag_far(s) for s in range(seqs)]
    near = [ag_near(s) for s in range(seqs)]
    for copy in far[0]:
        copy.start()
    near[0].start()

    def lane(h):
        return slice(h * HD, (h + 1) * HD)

    def pair_copy(src, dst, sem, s):
        return rc(src.at[s], dst.at[s], sem.at[0, s], sem.at[1, s], (pi, j))

    def group_copy(src, dst, ss, rs, s, to):
        return rc(src.at[s], dst.at[s, g], ss.at[s, to], rs.at[s, g], (2 * to + r, j))

    def spread(send, pair, total, slots, ps_, ss, rs, s, later):
        pair_copy(send, pair, ps_, s).wait_recv()
        for h in range(heads):
            total[s, h] = (send[s, h].astype(F32) + pair[s, h].astype(F32)).astype(BF16)
        for to in range(groups):
            @pl.when((to > g) if later else (to < g))
            def _():
                group_copy(total, slots, ss, rs, s, to).start()

    def spread_end(send, pair, total, slots, ps_, ss, rs, s, later):
        pair_copy(send, pair, ps_, s).wait_send()
        for to in range(groups):
            @pl.when((to > g) if later else (to < g))
            def _():
                group_copy(total, slots, ss, rs, s, to).wait_send()

    def gather_state(pair, slots, ss, rs, total, s, earlier):
        for h in range(heads):
            state[h] = jnp.where(r == (1 if earlier else 0), pair[s, h].astype(F32), 0.0)
        for frm in range(groups):
            @pl.when((frm < g) if earlier else (frm > g))
            def _():
                rc(total.at[s], slots.at[s, frm], ss.at[s, frm], rs.at[s, frm], (pi, j)).wait_recv()
                for h in range(heads):
                    state[h] += slots[s, frm, h].astype(F32)

    kargs = (ks_send, ks_pair, ks_sum, ks_slots, kp, kg_s, kg_r)
    qargs = (qs_send, qs_pair, qs_sum, qs_slots, qp, qg_s, qg_r)

    loads[0].wait()
    loads[1].wait()
    for s in range(seqs):
        for h in range(heads):
            ks_send[s, h] = dot(k_v[s, :, lane(h)], v_v[s, :, lane(h)], 0, 0).astype(BF16)
        pair_copy(ks_send, ks_pair, kp, s).start()

    rows = lax.broadcasted_iota(jnp.int32, (span, span), 0)
    causal = rows >= lax.broadcasted_iota(jnp.int32, (span, span), 1)

    loads[2].wait()
    for s in range(seqs):
        for h in range(heads):
            score = dot(q_v[s, :, lane(h)], k_v[s, :, lane(h)], 1, 1)
            score = jnp.where(causal, score, 0.0).astype(BF16)
            sc[s, h] = score
            att[s, :, lane(h)] = dot(score, v_v[s, :, lane(h)], 1, 0)
        spread(*kargs, s, True)
    loads[3].wait()
    loads[4].wait()

    def gated(s, src, first=False):
        at = pl.ds(pl.multiple_of(src * feat, feat), feat)
        new = dot(gbuf[s, src], wo_v[:, at], 1, 1)
        if first:
            dgated[...] = new
        else:
            dgated[...] += new

    def stage_b(s):
        own_loads[s].wait()
        gated(s, j, True)
        ag_wait(s, pj)
        gated(s, pj)
        if s + 1 < seqs:
            for copy in far[s]:
                copy.wait_send()
            for copy in far[s + 1]:
                copy.start()
            near[s + 1].start()
        for x, o in enumerate(others):
            src = 2 * o + p
            ag_wait(s, src)
            rc(gbuf.at[s, src], gbuf.at[s, src], ag_f.at[s, x], ag_r.at[s, src], (i, pj)).start()
            gated(s, src)
        for o in others:
            src = 2 * o + 1 - p
            ag_wait(s, src)
            gated(s, src)
        for h in range(heads):
            gate = jax.nn.sigmoid(g_v[s, :, lane(h)].astype(F32))
            d_out = (dgated[:, lane(h)] * gate).astype(BF16)
            dout[s, :, lane(h)] = d_out
            qs_send[s, h] = dot(q_v[s, :, lane(h)], d_out, 0, 0).astype(BF16)
        pair_copy(qs_send, qs_pair, qp, s).start()
        gather_state(ks_pair, ks_slots, kg_s, kg_r, ks_sum, s, True)
        for h in range(heads):
            query, key, value = q_v[s, :, lane(h)], k_v[s, :, lane(h)], v_v[s, :, lane(h)]
            d_out = dout[s, :, lane(h)]
            back = jnp.where(causal, dot(d_out, value, 1, 1), 0.0).astype(BF16)
            prefix = state[h].astype(BF16)
            dq = dot(back, key, 1, 0) + dot(d_out, prefix, 1, 1)
            dcat[0, s, :, lane(h)] = (factor * dq).astype(BF16)
            dki[s, :, lane(h)] = dot(back, query, 0, 0)
            dvi[s, :, lane(h)] = dot(sc[s, h], d_out, 0, 0)
            attended = factor * (att[s, :, lane(h)] + dot(query, prefix, 1, 0))
            gate = jax.nn.sigmoid(g_v[s, :, lane(h)].astype(F32))
            d_gate = dgated[:, lane(h)] * attended * gate * (1.0 - gate)
            dcat[1, s, :, lane(h)] = d_gate.astype(BF16)
        spread(*qargs, s, False)

    def half(s, at, lo):
        return dot(dcat[lo, s], w_v[lo, at, :], 1, 1) + dot(dcat[lo + 1, s], w_v[lo + 1, at, :], 1, 1)

    def early(s):
        def step(t, carry):
            at = pl.ds(pl.multiple_of(t * TILE, TILE), TILE)
            acc[:, at] = half(s, at, 0)
            return carry

        lax.fori_loop(0, width // TILE, step, 0)

    def tiles(s, chunk, started, put):
        def step(t, carry):
            at = pl.ds(pl.multiple_of(chunk * feat + t * TILE, TILE), TILE)
            to = pl.ds(pl.multiple_of(t * TILE, TILE), TILE)
            new = half(s, at, 2)
            put(to, new + (acc[:, at] if started else half(s, at, 0)))
            return carry

        lax.fori_loop(0, feat // TILE, step, 0)

    def part_copy(s, o):
        return rc(part_send.at[s, o], part_recv.at[s, o], ps.at[s, o], pr.at[s, o], (i, pj))

    def y_copy(s, o):
        return rc(y_send.at[s, o], y_recv.at[s, c], ys.at[s, o], yr.at[s, c], (i, 2 * o + p))

    def stage_c(s, started):
        gather_state(qs_pair, qs_slots, qg_s, qg_r, qs_sum, s, False)
        for h in range(heads):
            suffix = state[h].astype(BF16)
            dk = dki[s, :, lane(h)] + dot(v_v[s, :, lane(h)], suffix, 1, 1)
            dv = dvi[s, :, lane(h)] + dot(k_v[s, :, lane(h)], suffix, 1, 0)
            dcat[2, s, :, lane(h)] = (factor * dk).astype(BF16)
            dcat[3, s, :, lane(h)] = (factor * dv).astype(BF16)
        for o in others:
            def put(to, new):
                part_send[s, o, :, to] = new.astype(BF16)

            tiles(s, 2 * o + 1 - p, started, put)
            part_copy(s, o).start()
        for o in others:
            part_copy(s, o).wait_recv()

            def put(to, new):
                y_send[s, o, :, to] = (new + part_recv[s, o, :, to].astype(F32)).astype(BF16)

            tiles(s, 2 * o + p, started, put)
            y_copy(s, o).start()

        def put(to, new):
            part_send[s, c, :, to] = new.astype(BF16)

        tiles(s, 2 * c + 1 - p, started, put)
        part_copy(s, c).start()

        def put_own(to, new):
            own[s, :, to] = new

        tiles(s, j, started, put_own)

    def finish(s):
        part_copy(s, c).wait_recv()
        own[s] += part_recv[s, c].astype(F32)
        for o in others:
            rc(y_send.at[s, o], y_recv.at[s, o], ys.at[s, o], yr.at[s, o], (i, 2 * o + p)).wait_recv()
            own[s] += y_recv[s, o].astype(F32)
        out_ref[s] = own[s].astype(BF16)

    stage_b(0)
    for load in loads[5:]:
        load.wait()
    early(0)
    for s in range(1, seqs):
        stage_b(s)
    for s in range(seqs):
        stage_c(s, s == 0)
    for s in range(seqs):
        finish(s)

    for copy in far[seqs - 1]:
        copy.wait_send()
    for s in range(seqs):
        near[s].wait_send()
        for x, o in enumerate(others):
            src = 2 * o + p
            rc(gbuf.at[s, src], gbuf.at[s, src], ag_f.at[s, x], ag_r.at[s, src], (i, pj)).wait_send()
        spread_end(*kargs, s, True)
        spread_end(*qargs, s, False)
        for o in others:
            part_copy(s, o).wait_send()
            y_copy(s, o).wait_send()
        part_copy(s, c).wait_send()


def body(n, ns, queries, keys, values, gate_pre, grad_out, w_query, w_key, w_value, w_gate, w_out):
    seqs, span, cols = queries.shape
    feat, width = grad_out.shape[2], w_query.shape[0]
    heads, chips, groups = cols // HD, n // 2, ns // 2
    vm = pltpu.VMEM
    dma = pltpu.SemaphoreType.DMA
    tok = (seqs, span, cols)
    st = (seqs, heads, HD, HD)
    slots = (seqs, groups, heads, HD, HD)
    chunk = (seqs, chips, span, feat)
    scratch = [
        vm(tok, BF16), vm(tok, BF16), vm(tok, BF16), vm(tok, BF16),
        vm(w_out.shape, BF16), vm((4, width, cols), BF16),
        vm((seqs, n, span, feat), BF16),
        vm((seqs, heads, span, span), BF16), vm(tok, F32), vm((span, cols), F32),
        vm(tok, BF16), vm((4,) + tok, BF16), vm(tok, F32), vm(tok, F32), vm((span, width), F32),
        vm(st, BF16), vm(st, BF16), vm(st, BF16), vm(slots, BF16),
        vm(st, BF16), vm(st, BF16), vm(st, BF16), vm(slots, BF16),
        vm((heads, HD, HD), F32),
        vm(chunk, BF16), vm(chunk, BF16), vm(chunk, BF16), vm(chunk, BF16),
        vm((seqs, span, feat), F32),
        dma((9,)), dma((seqs,)), dma((seqs, chips)), dma((seqs, chips)), dma((seqs, n)),
        dma((2, seqs)), dma((seqs, groups)), dma((seqs, groups)),
        dma((2, seqs)), dma((seqs, groups)), dma((seqs, groups)),
        dma((seqs, chips)), dma((seqs, chips)), dma((seqs, chips)), dma((seqs, chips)),
    ]
    flops = 2 * seqs * span * cols * width * 5
    return pl.pallas_call(
        functools.partial(kernel, n, ns),
        out_shape=jax.ShapeDtypeStruct((seqs, span, feat), BF16),
        in_specs=[pl.BlockSpec(memory_space=pl.ANY)] * 10,
        out_specs=pl.BlockSpec(memory_space=pltpu.VMEM),
        scratch_shapes=scratch,
        cost_estimate=pl.CostEstimate(flops=flops, bytes_accessed=10 * width * cols, transcendentals=0),
        compiler_params=pltpu.CompilerParams(
            collective_id=0, has_side_effects=True, vmem_limit_bytes=58 * 1024 * 1024
        ),
    )(queries, keys, values, gate_pre, grad_out, w_query, w_key, w_value, w_gate, w_out)


def solution(mesh):
    return jax.shard_map(
        functools.partial(body, mesh.shape["head"], mesh.shape["seq"]),
        mesh=mesh,
        in_specs=(
            P(None, "seq", "head"),
            P(None, "seq", "head"),
            P(None, "seq", "head"),
            P(None, "seq", "head"),
            P(None, "seq", "head"),
            P(None, "head"),
            P(None, "head"),
            P(None, "head"),
            P(None, "head"),
            P("head", None),
        ),
        out_specs=P(None, "seq", "head"),
        check_vma=False,
    )
```

time: 235 us -> 75.4 us (0.32)
  the two profiles are of different devices: /device:TPU:0 before, /device:TPU:17 now
where the time goes in v1:
time: 75.4 us; the launch traced here: 75.3 us
  Pallas kernels  73 us (97%)
  local copies, waits for them, and re-layouts  2.26 us (3%)
    pallas_call x1, Pallas kernels, body(): pl.pallas_call(functools.partial(kernel, n, ns), out_shape=jax.ShapeDtype...  73 us
    unnamed x1, local copies, waits for them, and re-layouts  2.26 us

profile of v1, /device:TPU:17, one launch (start us, length us, event | category | flops | bytes accessed | tf_op | source)
XLA Modules:
  0.0 75.3 jit_solution(13101127729060027679)
XLA Ops:
  0.0 73.0 %shard_map.100 = bf16[2,256,1024]{2,1,0:T(8,128)(2,1)} custom-call(bf16[2,256,512]{2,1,0:T(8,128)(2,1)} %q_h.1, bf16[2,256,512]{2,1,0:T(8,128)(2,1)} %k_h.1, bf16[2,256,512]{2,1,0:T(8,128)(2,1)} %v_h.1, bf16[2,256,512]{2,1,0:T(8,128)(2,1)} %g_h.1, bf16[2,256,1024]{2,1,0:T(8,128)(2,1)} %go_h.1, bf16[4096,512]{1,0:T(8,128)(2,1)} %wq_h.1, ...), custom_call_target="tpu_custom_call" | custom-call | flops 10737418240 | bytes 20971520 | tf_op jit(solution)/shard_map/pallas_call | solution.py:309
  73.0 2.3 %copy.12 = bf16[2,256,1024]{2,1,0:T(8,128)(2,1)} copy(bf16[2,256,1024]{2,1,0:T(8,128)(2,1)} %shard_map.100) | data formatting | bytes 2097152

commit v2 on v1

v2 whole, which is shorter than its diff:
```python
import functools

import jax
import jax.numpy as jnp
from jax import lax
from jax.experimental import pallas as pl
from jax.experimental.pallas import tpu as pltpu
from jax.sharding import PartitionSpec as P

HD = 128
TILE = 256
MESH = pl.DeviceIdType.MESH
BF16, F32 = jnp.bfloat16, jnp.float32


def dot(a, b, ca, cb):
    return lax.dot_general(a, b, (((ca,), (cb,)), ((), ())), preferred_element_type=F32)


def kernel(
    n, ns,
    q_h, k_h, v_h, g_h, go_h, wq_h, wk_h, wv_h, wg_h, wo_h, own_h, y_h,
    q_v, k_v, v_v, g_v, wo_v, w_v, gbuf, sc, att, dgated, dout, dcat, dki, dvi, acc,
    ks_send, ks_pair, ks_sum, ks_slots, ks_z, qs_send, qs_pair, qs_sum, qs_slots, qs_z, state,
    part_send, part_recv, y_send, own, own_b,
    ld, ld_own, ag_s, ag_f, ag_r, kp, kg_s, kg_r, kz, qp, qg_s, qg_r, qz, ps, pr, ys, yr, ow,
):
    seqs, span, cols = q_v.shape
    feat = go_h.shape[2]
    width = wq_h.shape[0]
    heads = cols // HD
    hs = heads // 2
    chips, groups = n // 2, ns // 2
    factor = float(ns * span) ** (-0.5)
    i, j = lax.axis_index("seq"), lax.axis_index("head")
    c, p = j // 2, lax.rem(j, 2)
    g, r = i // 2, lax.rem(i, 2)
    pj, pi = j + 1 - 2 * p, i + 1 - 2 * r
    others = [lax.rem(c + d, chips) for d in range(1, chips)]

    def rc(src, dst, ss, rs, dev):
        return pltpu.make_async_remote_copy(
            src_ref=src, dst_ref=dst, send_sem=ss, recv_sem=rs, device_id=dev, device_id_type=MESH
        )

    barrier = pltpu.get_barrier_semaphore()
    peers = [(i, pj), (pi, j)]
    peers += [(i, 2 * o + p) for o in others]
    peers += [(2 * lax.rem(g + d, groups) + r, j) for d in range(1, groups)]
    for peer in peers:
        pl.semaphore_signal(barrier, inc=1, device_id=peer, device_id_type=MESH)

    pairs = [(k_h, k_v), (v_h, v_v), (q_h, q_v), (wo_h, wo_v), (g_h, g_v)]
    pairs += [(w, w_v.at[x]) for x, w in enumerate((wq_h, wg_h, wk_h, wv_h))]
    loads = [pltpu.make_async_copy(a, b, ld.at[x]) for x, (a, b) in enumerate(pairs)]
    own_loads = [pltpu.make_async_copy(go_h.at[s], gbuf.at[s, j], ld_own.at[s]) for s in range(seqs)]
    for load in loads[:4] + own_loads + loads[4:]:
        load.start()
    pl.semaphore_wait(barrier, len(peers))

    def ag_far(s):
        return [
            rc(go_h.at[s], gbuf.at[s, j], ag_s.at[s, x], ag_r.at[s, j], (i, 2 * o + p))
            for x, o in enumerate(others)
        ]

    def ag_near(s):
        return rc(go_h.at[s], gbuf.at[s, j], ag_s.at[s, chips - 1], ag_r.at[s, j], (i, pj))

    def ag_wait(s, src):
        rc(go_h.at[s], gbuf.at[s, src], ag_s.at[s, 0], ag_r.at[s, src], (i, pj)).wait_recv()

    far = [ag_far(s) for s in range(seqs)]
    near = [ag_near(s) for s in range(seqs)]
    for copy in far[0]:
        copy.start()
    near[0].start()

    def lane(h):
        return slice(h * HD, (h + 1) * HD)

    def pair_copy(a, s, m):
        half = r if m else 1 - r
        return rc(a[0].at[s, half], a[1].at[s, half], a[5].at[0, s, m], a[5].at[1, s, m], (pi, j))

    def group_copy(a, s, to):
        return rc(a[2].at[s], a[3].at[s, g], a[6].at[s, to], a[7].at[s, g], (2 * to + r, j))

    def z_copy(a, s):
        return rc(a[4].at[s, r], a[4].at[s, r], a[8].at[0, s], a[8].at[1, s], (pi, j))

    def send_pair(a, s):
        pair_copy(a, s, 0).start()
        pair_copy(a, s, 1).start()

    def relay_p(a, s):
        pair_copy(a, s, 0).wait_recv()
        for k in range(hs):
            a[2][s, k] = (a[0][s, r, k].astype(F32) + a[1][s, r, k].astype(F32)).astype(BF16)
        for to in range(groups):
            @pl.when((to > g) if a[9] else (to < g))
            def _():
                group_copy(a, s, to).start()

    def relay_z(a, s):
        for k in range(hs):
            state[k] = jnp.zeros((HD, HD), F32)
        for frm in range(groups):
            @pl.when((frm < g) if a[9] else (frm > g))
            def _():
                rc(a[2].at[s], a[3].at[s, frm], a[6].at[s, frm], a[7].at[s, frm], (pi, j)).wait_recv()
                for k in range(hs):
                    state[k] += a[3][s, frm, k].astype(F32)
        for k in range(hs):
            a[4][s, r, k] = state[k].astype(BF16)
        z_copy(a, s).start()

    def gather_state(a, s):
        pair_copy(a, s, 1).wait_recv()
        rc(a[4].at[s, 1 - r], a[4].at[s, 1 - r], a[8].at[0, s], a[8].at[1, s], (pi, j)).wait_recv()
        for h in range(heads):
            at = (s, h // hs, h % hs)
            near_state = jnp.where(r == (1 if a[9] else 0), a[1][at].astype(F32), 0.0)
            state[h] = a[4][at].astype(F32) + near_state

    def end_state(a, s):
        pair_copy(a, s, 0).wait_send()
        pair_copy(a, s, 1).wait_send()
        z_copy(a, s).wait_send()
        for to in range(groups):
            @pl.when((to > g) if a[9] else (to < g))
            def _():
                group_copy(a, s, to).wait_send()

    ka = (ks_send, ks_pair, ks_sum, ks_slots, ks_z, kp, kg_s, kg_r, kz, True)
    qa = (qs_send, qs_pair, qs_sum, qs_slots, qs_z, qp, qg_s, qg_r, qz, False)

    loads[0].wait()
    loads[1].wait()
    for s in range(seqs):
        for h in range(heads):
            ks_send[s, h // hs, h % hs] = dot(k_v[s, :, lane(h)], v_v[s, :, lane(h)], 0, 0).astype(BF16)
        send_pair(ka, s)

    rows = lax.broadcasted_iota(jnp.int32, (span, span), 0)
    causal = rows >= lax.broadcasted_iota(jnp.int32, (span, span), 1)

    loads[2].wait()
    for s in range(seqs):
        for h in range(heads):
            score = dot(q_v[s, :, lane(h)], k_v[s, :, lane(h)], 1, 1)
            score = jnp.where(causal, score, 0.0).astype(BF16)
            sc[s, h] = score
            att[s, :, lane(h)] = dot(score, v_v[s, :, lane(h)], 1, 0)
        relay_p(ka, s)
    loads[3].wait()
    loads[4].wait()

    def gated(s, src, first=False):
        at = pl.ds(pl.multiple_of(src * feat, feat), feat)
        new = dot(gbuf[s, src], wo_v[:, at], 1, 1)
        if first:
            dgated[...] = new
        else:
            dgated[...] += new

    def gate_stage(s, hook):
        own_loads[s].wait()
        gated(s, j, True)
        ag_wait(s, pj)
        gated(s, pj)
        if s + 1 < seqs:
            for copy in far[s]:
                copy.wait_send()
            for copy in far[s + 1]:
                copy.start()
            near[s + 1].start()
        for x, o in enumerate(others):
            src = 2 * o + p
            ag_wait(s, src)
            rc(gbuf.at[s, src], gbuf.at[s, src], ag_f.at[s, x], ag_r.at[s, src], (i, pj)).start()
            gated(s, src)
        hook()
        for o in others:
            src = 2 * o + 1 - p
            ag_wait(s, src)
            gated(s, src)
        for h in range(heads):
            gate = jax.nn.sigmoid(g_v[s, :, lane(h)].astype(F32))
            d_out = (dgated[:, lane(h)] * gate).astype(BF16)
            dout[s, :, lane(h)] = d_out
            qs_send[s, h // hs, h % hs] = dot(q_v[s, :, lane(h)], d_out, 0, 0).astype(BF16)
        send_pair(qa, s)

    def head_stage(s, hook):
        gather_state(ka, s)
        for h in range(heads):
            if h == hs:
                hook()
            query, key, value = q_v[s, :, lane(h)], k_v[s, :, lane(h)], v_v[s, :, lane(h)]
            d_out = dout[s, :, lane(h)]
            back = jnp.where(causal, dot(d_out, value, 1, 1), 0.0).astype(BF16)
            prefix = state[h].astype(BF16)
            dq = dot(back, key, 1, 0) + dot(d_out, prefix, 1, 1)
            dcat[0, s, :, lane(h)] = (factor * dq).astype(BF16)
            dki[s, :, lane(h)] = dot(back, query, 0, 0)
            dvi[s, :, lane(h)] = dot(sc[s, h], d_out, 0, 0)
            attended = factor * (att[s, :, lane(h)] + dot(query, prefix, 1, 0))
            gate = jax.nn.sigmoid(g_v[s, :, lane(h)].astype(F32))
            d_gate = dgated[:, lane(h)] * attended * gate * (1.0 - gate)
            dcat[1, s, :, lane(h)] = d_gate.astype(BF16)

    def half(s, at, lo):
        return dot(dcat[lo, s], w_v[lo, at, :], 1, 1) + dot(dcat[lo + 1, s], w_v[lo + 1, at, :], 1, 1)

    def early(s):
        def step(t, carry):
            at = pl.ds(pl.multiple_of(t * TILE, TILE), TILE)
            acc[:, at] = half(s, at, 0)
            return carry

        lax.fori_loop(0, width // TILE, step, 0)

    def tiles(s, chunk, put):
        def step(t, carry):
            at = pl.ds(pl.multiple_of(chunk * feat + t * TILE, TILE), TILE)
            to = pl.ds(pl.multiple_of(t * TILE, TILE), TILE)
            put(to, half(s, at, 2) + acc[:, at])
            return carry

        lax.fori_loop(0, feat // TILE, step, 0)

    def part_copy(s, o):
        return rc(part_send.at[s, o], part_recv.at[s, o], ps.at[s, o], pr.at[s, o], (i, pj))

    def y_copy(s, d):
        o = others[d - 1]
        to = chips - d - 1
        return rc(y_send.at[s, d - 1], y_h.at[to, s], ys.at[s, d - 1], yr.at[s, to], (i, 2 * o + p))

    def for_partner(s, o):
        def put(to, new):
            part_send[s, o, :, to] = new.astype(BF16)

        tiles(s, 2 * o + 1 - p, put)
        part_copy(s, o).start()

    def far_stage(s, hook):
        gather_state(qa, s)
        for h in range(heads):
            suffix = state[h].astype(BF16)
            dk = dki[s, :, lane(h)] + dot(v_v[s, :, lane(h)], suffix, 1, 1)
            dv = dvi[s, :, lane(h)] + dot(k_v[s, :, lane(h)], suffix, 1, 0)
            dcat[2, s, :, lane(h)] = (factor * dk).astype(BF16)
            dcat[3, s, :, lane(h)] = (factor * dv).astype(BF16)
        for o in others:
            for_partner(s, o)
        hook()
        for d in range(1, chips):
            o = others[d - 1]
            part_copy(s, o).wait_recv()

            def put(to, new):
                y_send[s, d - 1, :, to] = (new + part_recv[s, o, :, to].astype(F32)).astype(BF16)

            tiles(s, 2 * o + p, put)
            y_copy(s, d).start()

    def near_stage(s):
        for_partner(s, c)

        def put(to, new):
            own[s, :, to] = new

        tiles(s, j, put)

    def own_copy(s):
        return pltpu.make_async_copy(own_b.at[s], own_h.at[s], ow.at[s])

    def finish(s):
        part_copy(s, c).wait_recv()
        own_b[s] = (own[s] + part_recv[s, c].astype(F32)).astype(BF16)
        own_copy(s).start()

    gate_stage(0, lambda: relay_z(ka, 0))
    head_stage(0, lambda: relay_p(qa, 0))
    relay_z(ka, 1)
    for load in loads[5:]:
        load.wait()
    early(0)
    gate_stage(1, lambda: relay_z(qa, 0))
    far_stage(0, lambda: relay_p(qa, 1))
    head_stage(1, lambda: None)
    relay_z(qa, 1)
    near_stage(0)
    early(1)
    far_stage(1, lambda: None)
    near_stage(1)
    finish(0)
    finish(1)

    for copy in far[seqs - 1]:
        copy.wait_send()
    for s in range(seqs):
        near[s].wait_send()
        for x, o in enumerate(others):
            src = 2 * o + p
            rc(gbuf.at[s, src], gbuf.at[s, src], ag_f.at[s, x], ag_r.at[s, src], (i, pj)).wait_send()
        end_state(ka, s)
        end_state(qa, s)
        for o in others:
            part_copy(s, o).wait_send()
        part_copy(s, c).wait_send()
        own_copy(s).wait()
        for d in range(1, chips):
            y_copy(s, d).wait_send()
            rc(y_send.at[s, d - 1], y_h.at[d - 1, s], ys.at[s, d - 1], yr.at[s, d - 1], (i, pj)).wait_recv()


def body(n, ns, queries, keys, values, gate_pre, grad_out, w_query, w_key, w_value, w_gate, w_out):
    seqs, span, cols = queries.shape
    feat, width = grad_out.shape[2], w_query.shape[0]
    heads, chips, groups = cols // HD, n // 2, ns // 2
    vm = pltpu.VMEM
    dma = pltpu.SemaphoreType.DMA
    tok = (seqs, span, cols)
    st = (seqs, 2, heads // 2, HD, HD)
    one = (seqs, heads // 2, HD, HD)
    slots = (seqs, groups, heads // 2, HD, HD)
    chunk = (seqs, chips, span, feat)
    scratch = [
        vm(tok, BF16), vm(tok, BF16), vm(tok, BF16), vm(tok, BF16),
        vm(w_out.shape, BF16), vm((4, width, cols), BF16),
        vm((seqs, n, span, feat), BF16),
        vm((seqs, heads, span, span), BF16), vm(tok, F32), vm((span, cols), F32),
        vm(tok, BF16), vm((4,) + tok, BF16), vm(tok, F32), vm(tok, F32), vm((span, width), F32),
        vm(st, BF16), vm(st, BF16), vm(one, BF16), vm(slots, BF16), vm(st, BF16),
        vm(st, BF16), vm(st, BF16), vm(one, BF16), vm(slots, BF16), vm(st, BF16),
        vm((heads, HD, HD), F32),
        vm(chunk, BF16), vm(chunk, BF16), vm((seqs, chips - 1, span, feat), BF16),
        vm((seqs, span, feat), F32), vm((seqs, span, feat), BF16),
        dma((9,)), dma((seqs,)), dma((seqs, chips)), dma((seqs, chips)), dma((seqs, n)),
        dma((2, seqs, 2)), dma((seqs, groups)), dma((seqs, groups)), dma((2, seqs)),
        dma((2, seqs, 2)), dma((seqs, groups)), dma((seqs, groups)), dma((2, seqs)),
        dma((seqs, chips)), dma((seqs, chips)), dma((seqs, chips)), dma((seqs, chips)), dma((seqs,)),
    ]
    flops = 2 * seqs * span * cols * width * 5
    own, far = pl.pallas_call(
        functools.partial(kernel, n, ns),
        out_shape=(
            jax.ShapeDtypeStruct((seqs, span, feat), BF16),
            jax.ShapeDtypeStruct((chips - 1, seqs, span, feat), BF16),
        ),
        in_specs=[pl.BlockSpec(memory_space=pl.ANY)] * 10,
        out_specs=[pl.BlockSpec(memory_space=pl.ANY)] * 2,
        scratch_shapes=scratch,
        cost_estimate=pl.CostEstimate(flops=flops, bytes_accessed=10 * width * cols, transcendentals=0),
        compiler_params=pltpu.CompilerParams(
            collective_id=0, has_side_effects=True, vmem_limit_bytes=58 * 1024 * 1024
        ),
    )(queries, keys, values, gate_pre, grad_out, w_query, w_key, w_value, w_gate, w_out)
    total = own.astype(F32)
    for d in range(chips - 1):
        total = total + far[d].astype(F32)
    return total.astype(BF16)


def solution(mesh):
    return jax.shard_map(
        functools.partial(body, mesh.shape["head"], mesh.shape["seq"]),
        mesh=mesh,
        in_specs=(
            P(None, "seq", "head"),
            P(None, "seq", "head"),
            P(None, "seq", "head"),
            P(None, "seq", "head"),
            P(None, "seq", "head"),
            P(None, "head"),
            P(None, "head"),
            P(None, "head"),
            P(None, "head"),
            P("head", None),
        ),
        out_specs=P(None, "seq", "head"),
        check_vma=False,
    )
```

time: 75.4 us -> 72.2 us (0.958)
  the two profiles are of different devices: /device:TPU:17 before, /device:TPU:0 now
where the time goes in v2:
time: 72.2 us; the launch traced here: 72.1 us
  Pallas kernels  69.2 us (96%)
  other arithmetic  2.92 us (4%)
    pallas_call x1, Pallas kernels, body(): pl.pallas_call(functools.partial(kernel, n, ns), out_shape=(jax.ShapeDtyp...  69.2 us
    convert_element_type x1, other arithmetic, body(): return total.astype(BF16)  2.92 us

profile of v2, /device:TPU:0, one launch (start us, length us, event | category | flops | bytes accessed | tf_op | source)
XLA Modules:
  0.0 72.1 jit_solution(5950549964385490588)
XLA Ops:
  0.0 69.2 %shard_map.100 = (bf16[2,256,1024]{2,1,0:T(8,128)(2,1)}, bf16[1,2,256,1024]{3,2,1,0:T(8,128)(2,1)}) custom-call(bf16[2,256,512]{2,1,0:T(8,128)(2,1)} %q_h.1, bf16[2,256,512]{2,1,0:T(8,128)(2,1)} %k_h.1, bf16[2,256,512]{2,1,0:T(8,128)(2,1)} %v_h.1, bf16[2,256,512]{2,1,0:T(8,128)(2,1)} %g_h.1, bf16[2,256,1024]{2,1,0:T(8,128)(2,1)} %go_h.1, ...), custom_call_target="tpu_custom_call" | custom-call | flops 10737418240 | bytes 20971520 | tf_op jit(solution)/shard_map/pallas_call | solution.py:348
  69.2 2.9 %fusion = bf16[2,256,1024]{2,1,0:T(8,128)(2,1)} fusion(bf16[2,256,1024]{2,1,0:T(8,128)(2,1)} %get-tuple-element.7, bf16[1,2,256,1024]{3,2,1,0:T(8,128)(2,1)} %get-tuple-element.8), kind=kLoop, calls=%fused_computation.1 | loop fusion | flops 2097152 | bytes 3145728 | tf_op jit(solution)/shard_map/convert_element_type | solution.py:365

commit v3 on v2

--- a/solution.py
+++ b/solution.py
@@ -8,7 +8,7 @@
 from jax.sharding import PartitionSpec as P
 
 HD = 128
-TILE = 256
+TILE = 512
 MESH = pl.DeviceIdType.MESH
 BF16, F32 = jnp.bfloat16, jnp.float32
 
@@ -51,7 +51,7 @@
         pl.semaphore_signal(barrier, inc=1, device_id=peer, device_id_type=MESH)
 
     pairs = [(k_h, k_v), (v_h, v_v), (q_h, q_v), (wo_h, wo_v), (g_h, g_v)]
-    pairs += [(w, w_v.at[x]) for x, w in enumerate((wq_h, wg_h, wk_h, wv_h))]
+    pairs += [(w, w_v.at[:, pl.ds(x * cols, cols)]) for x, w in enumerate((wq_h, wg_h, wk_h, wv_h))]
     loads = [pltpu.make_async_copy(a, b, ld.at[x]) for x, (a, b) in enumerate(pairs)]
     own_loads = [pltpu.make_async_copy(go_h.at[s], gbuf.at[s, j], ld_own.at[s]) for s in range(seqs)]
     for load in loads[:4] + own_loads + loads[4:]:
@@ -164,7 +164,7 @@
         else:
             dgated[...] += new
 
-    def gate_stage(s, hook):
+    def gate_stage(s, before, sent, after):
         own_loads[s].wait()
         gated(s, j, True)
         ag_wait(s, pj)
@@ -175,12 +175,15 @@
             for copy in far[s + 1]:
                 copy.start()
             near[s + 1].start()
+        before()
         for x, o in enumerate(others):
             src = 2 * o + p
             ag_wait(s, src)
             rc(gbuf.at[s, src], gbuf.at[s, src], ag_f.at[s, x], ag_r.at[s, src], (i, pj)).start()
-            gated(s, src)
-        hook()
+        sent()
+        for o in others:
+            gated(s, 2 * o + p)
+        after()
         for o in others:
             src = 2 * o + 1 - p
             ag_wait(s, src)
@@ -202,77 +205,93 @@
             back = jnp.where(causal, dot(d_out, value, 1, 1), 0.0).astype(BF16)
             prefix = state[h].astype(BF16)
             dq = dot(back, key, 1, 0) + dot(d_out, prefix, 1, 1)
-            dcat[0, s, :, lane(h)] = (factor * dq).astype(BF16)
+            dcat[s, :, lane(0 * heads + h)] = (factor * dq).astype(BF16)
             dki[s, :, lane(h)] = dot(back, query, 0, 0)
             dvi[s, :, lane(h)] = dot(sc[s, h], d_out, 0, 0)
             attended = factor * (att[s, :, lane(h)] + dot(query, prefix, 1, 0))
             gate = jax.nn.sigmoid(g_v[s, :, lane(h)].astype(F32))
             d_gate = dgated[:, lane(h)] * attended * gate * (1.0 - gate)
-            dcat[1, s, :, lane(h)] = d_gate.astype(BF16)
-
-    def half(s, at, lo):
-        return dot(dcat[lo, s], w_v[lo, at, :], 1, 1) + dot(dcat[lo + 1, s], w_v[lo + 1, at, :], 1, 1)
-
-    def early(s):
-        def step(t, carry):
-            at = pl.ds(pl.multiple_of(t * TILE, TILE), TILE)
-            acc[:, at] = half(s, at, 0)
+            dcat[s, :, lane(1 * heads + h)] = d_gate.astype(BF16)
+
+    tile = min(TILE, feat // 2)
+
+    def product(s, at, lo, hi):
+        lo, hi = lo * cols, hi * cols
+        return dot(dcat[s, :, lo:hi], w_v[at, lo:hi], 1, 1)
+
+    def tile_loop(step):
+        def run(t, carry):
+            step(t)
             return carry
 
-        lax.fori_loop(0, width // TILE, step, 0)
-
-    def tiles(s, chunk, put):
-        def step(t, carry):
-            at = pl.ds(pl.multiple_of(chunk * feat + t * TILE, TILE), TILE)
-            to = pl.ds(pl.multiple_of(t * TILE, TILE), TILE)
-            put(to, half(s, at, 2) + acc[:, at])
-            return carry
-
-        lax.fori_loop(0, feat // TILE, step, 0)
+        lax.fori_loop(0, feat // tile, run, 0)
+
+    def early(s, chunk):
+        def step(t):
+            at = pl.ds(pl.multiple_of(chunk * feat + t * tile, tile), tile)
+            acc[:, at] = product(s, at, 0, 2)
+
+        tile_loop(step)
+
+    def tiles(s, chunk, put, whole=False):
+        def step(t):
+            at = pl.ds(pl.multiple_of(chunk * feat + t * tile, tile), tile)
+            to = pl.ds(pl.multiple_of(t * tile, tile), tile)
+            put(to, product(s, at, 0, 4) if whole else product(s, at, 2, 4) + acc[:, at])
+
+        tile_loop(step)
 
     def part_copy(s, o):
         return rc(part_send.at[s, o], part_recv.at[s, o], ps.at[s, o], pr.at[s, o], (i, pj))
 
-    def y_copy(s, d):
+    def y_copy(s, d, t):
         o = others[d - 1]
         to = chips - d - 1
-        return rc(y_send.at[s, d - 1], y_h.at[to, s], ys.at[s, d - 1], yr.at[s, to], (i, 2 * o + p))
-
-    def for_partner(s, o):
+        at = pl.ds(pl.multiple_of(t * tile, tile), tile)
+        return rc(
+            y_send.at[s, d - 1, :, at], y_h.at[to, s, :, at],
+            ys.at[s, d - 1, t], yr.at[s, to, t], (i, 2 * o + p),
+        )
+
+    def for_partner(s, o, whole=False):
         def put(to, new):
             part_send[s, o, :, to] = new.astype(BF16)
 
-        tiles(s, 2 * o + 1 - p, put)
+        tiles(s, 2 * o + 1 - p, put, whole)
         part_copy(s, o).start()
 
-    def far_stage(s, hook):
+    def far_begin(s):
         gather_state(qa, s)
         for h in range(heads):
             suffix = state[h].astype(BF16)
             dk = dki[s, :, lane(h)] + dot(v_v[s, :, lane(h)], suffix, 1, 1)
             dv = dvi[s, :, lane(h)] + dot(k_v[s, :, lane(h)], suffix, 1, 0)
-            dcat[2, s, :, lane(h)] = (factor * dk).astype(BF16)
-            dcat[3, s, :, lane(h)] = (factor * dv).astype(BF16)
+            dcat[s, :, lane(2 * heads + h)] = (factor * dk).astype(BF16)
+            dcat[s, :, lane(3 * heads + h)] = (factor * dv).astype(BF16)
         for o in others:
             for_partner(s, o)
-        hook()
+
+    def far_end(s):
         for d in range(1, chips):
             o = others[d - 1]
             part_copy(s, o).wait_recv()
 
-            def put(to, new):
-                y_send[s, d - 1, :, to] = (new + part_recv[s, o, :, to].astype(F32)).astype(BF16)
-
-            tiles(s, 2 * o + p, put)
-            y_copy(s, d).start()
-
-    def near_stage(s):
-        for_partner(s, c)
+            def step(t):
+                at = pl.ds(pl.multiple_of((2 * o + p) * feat + t * tile, tile), tile)
+                to = pl.ds(pl.multiple_of(t * tile, tile), tile)
+                new = product(s, at, 2, 4) + acc[:, at] + part_recv[s, o, :, to].astype(F32)
+                y_send[s, d - 1, :, to] = new.astype(BF16)
+                y_copy(s, d, t).start()
+
+            tile_loop(step)
+
+    def near_stage(s, whole):
+        for_partner(s, c, whole)
 
         def put(to, new):
             own[s, :, to] = new
 
-        tiles(s, j, put)
+        tiles(s, j, put, whole)
 
     def own_copy(s):
         return pltpu.make_async_copy(own_b.at[s], own_h.at[s], ow.at[s])
@@ -282,20 +301,27 @@
         own_b[s] = (own[s] + part_recv[s, c].astype(F32)).astype(BF16)
         own_copy(s).start()
 
-    gate_stage(0, lambda: relay_z(ka, 0))
+    def nothing():
+        return None
+
+    gate_stage(0, nothing, nothing, lambda: relay_z(ka, 0))
     head_stage(0, lambda: relay_p(qa, 0))
     relay_z(ka, 1)
     for load in loads[5:]:
         load.wait()
-    early(0)
-    gate_stage(1, lambda: relay_z(qa, 0))
-    far_stage(0, lambda: relay_p(qa, 1))
-    head_stage(1, lambda: None)
+    lax.fori_loop(0, n, lambda x, carry: (early(0, x), carry)[1], 0)
+    gate_stage(1, lambda: relay_z(qa, 0), lambda: far_begin(0), nothing)
+    far_end(0)
+    relay_p(qa, 1)
+    head_stage(1, nothing)
     relay_z(qa, 1)
-    near_stage(0)
-    early(1)
-    far_stage(1, lambda: None)
-    near_stage(1)
+    for o in others:
+        early(1, 2 * o + 1 - p)
+        early(1, 2 * o + p)
+    far_begin(1)
+    far_end(1)
+    near_stage(0, False)
+    near_stage(1, True)
     finish(0)
     finish(1)
 
@@ -313,8 +339,13 @@
         part_copy(s, c).wait_send()
         own_copy(s).wait()
         for d in range(1, chips):
-            y_copy(s, d).wait_send()
-            rc(y_send.at[s, d - 1], y_h.at[d - 1, s], ys.at[s, d - 1], yr.at[s, d - 1], (i, pj)).wait_recv()
+            for t in range(feat // tile):
+                y_copy(s, d, t).wait_send()
+                at = pl.ds(t * tile, tile)
+                rc(
+                    y_send.at[s, d - 1, :, at], y_h.at[d - 1, s, :, at],
+                    ys.at[s, d - 1, t], yr.at[s, d - 1, t], (i, pj),
+                ).wait_recv()
 
 
 def body(n, ns, queries, keys, values, gate_pre, grad_out, w_query, w_key, w_value, w_gate, w_out):
@@ -330,10 +361,10 @@
     chunk = (seqs, chips, span, feat)
     scratch = [
         vm(tok, BF16), vm(tok, BF16), vm(tok, BF16), vm(tok, BF16),
-        vm(w_out.shape, BF16), vm((4, width, cols), BF16),
+        vm(w_out.shape, BF16), vm((width, 4 * cols), BF16),
         vm((seqs, n, span, feat), BF16),
         vm((seqs, heads, span, span), BF16), vm(tok, F32), vm((span, cols), F32),
-        vm(tok, BF16), vm((4,) + tok, BF16), vm(tok, F32), vm(tok, F32), vm((span, width), F32),
+        vm(tok, BF16), vm((seqs, span, 4 * cols), BF16), vm(tok, F32), vm(tok, F32), vm((span, width), F32),
         vm(st, BF16), vm(st, BF16), vm(one, BF16), vm(slots, BF16), vm(st, BF16),
         vm(st, BF16), vm(st, BF16), vm(one, BF16), vm(slots, BF16), vm(st, BF16),
         vm((heads, HD, HD), F32),
@@ -342,7 +373,7 @@
         dma((9,)), dma((seqs,)), dma((seqs, chips)), dma((seqs, chips)), dma((seqs, n)),
         dma((2, seqs, 2)), dma((seqs, groups)), dma((seqs, groups)), dma((2, seqs)),
         dma((2, seqs, 2)), dma((seqs, groups)), dma((seqs, groups)), dma((2, seqs)),
-        dma((seqs, chips)), dma((seqs, chips)), dma((seqs, chips)), dma((seqs, chips)), dma((seqs,)),
+        dma((seqs, chips)), dma((seqs, chips)), dma((seqs, chips, 2)), dma((seqs, chips, 2)), dma((seqs,)),
     ]
     flops = 2 * seqs * span * cols * width * 5
     own, far = pl.pallas_call(

time: 72.2 us -> 67.3 us (0.932)
  Pallas kernels: 69.2 us -> 63.6 us
    pallas_call x1, Pallas kernels: 69.2 us -> 63.6 us  [body(): pl.pallas_call(functools.partial(kernel, n, ns), out_shape=(jax.ShapeDtyp...]
where the time goes in v3:
time: 67.3 us; the launch traced here: 66.5 us
  Pallas kernels  63.6 us (95%)
  other arithmetic  2.92 us (4%)
    pallas_call x1, Pallas kernels, body(): pl.pallas_call(functools.partial(kernel, n, ns), out_shape=(jax.ShapeDtyp...  63.6 us
    convert_element_type x1, other arithmetic, body(): return total.astype(BF16)  2.92 us

profile of v3, /device:TPU:0, one launch (start us, length us, event | category | flops | bytes accessed | tf_op | source)
XLA Modules:
  0.0 66.5 jit_solution(13075033876173736793)
XLA Ops:
  0.0 63.6 %shard_map.100 = (bf16[2,256,1024]{2,1,0:T(8,128)(2,1)}, bf16[1,2,256,1024]{3,2,1,0:T(8,128)(2,1)}) custom-call(bf16[2,256,512]{2,1,0:T(8,128)(2,1)} %q_h.1, bf16[2,256,512]{2,1,0:T(8,128)(2,1)} %k_h.1, bf16[2,256,512]{2,1,0:T(8,128)(2,1)} %v_h.1, bf16[2,256,512]{2,1,0:T(8,128)(2,1)} %g_h.1, bf16[2,256,1024]{2,1,0:T(8,128)(2,1)} %go_h.1, ...), custom_call_target="tpu_custom_call" | custom-call | flops 10737418240 | bytes 20971520 | tf_op jit(solution)/shard_map/pallas_call | solution.py:379
  63.6 2.9 %fusion = bf16[2,256,1024]{2,1,0:T(8,128)(2,1)} fusion(bf16[2,256,1024]{2,1,0:T(8,128)(2,1)} %get-tuple-element.7, bf16[1,2,256,1024]{3,2,1,0:T(8,128)(2,1)} %get-tuple-element.8), kind=kLoop, calls=%fused_computation.1 | loop fusion | flops 2097152 | bytes 3145728 | tf_op jit(solution)/shard_map/convert_element_type | solution.py:396

commit v4 on v3

--- a/solution.py
+++ b/solution.py
@@ -20,7 +20,7 @@
 def kernel(
     n, ns,
     q_h, k_h, v_h, g_h, go_h, wq_h, wk_h, wv_h, wg_h, wo_h, own_h, y_h,
-    q_v, k_v, v_v, g_v, wo_v, w_v, gbuf, sc, att, dgated, dout, dcat, dki, dvi, acc,
+    q_v, k_v, v_v, g_v, wo_v, w_v, gbuf, sct, q_t, att, dgated, dout, dcat, dki, dvi, acc,
     ks_send, ks_pair, ks_sum, ks_slots, ks_z, qs_send, qs_pair, qs_sum, qs_slots, qs_z, state,
     part_send, part_recv, y_send, own, own_b,
     ld, ld_own, ag_s, ag_f, ag_r, kp, kg_s, kg_r, kz, qp, qg_s, qg_r, qz, ps, pr, ys, yr, ow,
@@ -74,7 +74,8 @@
     near = [ag_near(s) for s in range(seqs)]
     for copy in far[0]:
         copy.start()
-    near[0].start()
+    for copy in near:
+        copy.start()
 
     def lane(h):
         return slice(h * HD, (h + 1) * HD)
@@ -143,14 +144,17 @@
         send_pair(ka, s)
 
     rows = lax.broadcasted_iota(jnp.int32, (span, span), 0)
-    causal = rows >= lax.broadcasted_iota(jnp.int32, (span, span), 1)
+    columns = lax.broadcasted_iota(jnp.int32, (span, span), 1)
+    causal, anti = rows >= columns, rows <= columns
 
     loads[2].wait()
     for s in range(seqs):
         for h in range(heads):
             score = dot(q_v[s, :, lane(h)], k_v[s, :, lane(h)], 1, 1)
             score = jnp.where(causal, score, 0.0).astype(BF16)
-            sc[s, h] = score
+            flip = dot(k_v[s, :, lane(h)], q_v[s, :, lane(h)], 1, 1)
+            sct[s, h] = jnp.where(anti, flip, 0.0).astype(BF16)
+            q_t[s, h] = q_v[s, :, lane(h)].T
             att[s, :, lane(h)] = dot(score, v_v[s, :, lane(h)], 1, 0)
         relay_p(ka, s)
     loads[3].wait()
@@ -160,21 +164,16 @@
         at = pl.ds(pl.multiple_of(src * feat, feat), feat)
         new = dot(gbuf[s, src], wo_v[:, at], 1, 1)
         if first:
-            dgated[...] = new
+            dgated[s] = new
         else:
-            dgated[...] += new
+            dgated[s] += new
 
     def gate_stage(s, before, sent, after):
-        own_loads[s].wait()
-        gated(s, j, True)
-        ag_wait(s, pj)
-        gated(s, pj)
         if s + 1 < seqs:
             for copy in far[s]:
                 copy.wait_send()
             for copy in far[s + 1]:
                 copy.start()
-            near[s + 1].start()
         before()
         for x, o in enumerate(others):
             src = 2 * o + p
@@ -190,9 +189,9 @@
             gated(s, src)
         for h in range(heads):
             gate = jax.nn.sigmoid(g_v[s, :, lane(h)].astype(F32))
-            d_out = (dgated[:, lane(h)] * gate).astype(BF16)
+            d_out = (dgated[s, :, lane(h)] * gate).astype(BF16)
             dout[s, :, lane(h)] = d_out
-            qs_send[s, h // hs, h % hs] = dot(q_v[s, :, lane(h)], d_out, 0, 0).astype(BF16)
+            qs_send[s, h // hs, h % hs] = dot(q_t[s, h], d_out, 1, 0).astype(BF16)
         send_pair(qa, s)
 
     def head_stage(s, hook):
@@ -206,11 +205,12 @@
             prefix = state[h].astype(BF16)
             dq = dot(back, key, 1, 0) + dot(d_out, prefix, 1, 1)
             dcat[s, :, lane(0 * heads + h)] = (factor * dq).astype(BF16)
-            dki[s, :, lane(h)] = dot(back, query, 0, 0)
-            dvi[s, :, lane(h)] = dot(sc[s, h], d_out, 0, 0)
+            flip = jnp.where(anti, dot(value, d_out, 1, 1), 0.0).astype(BF16)
+            dki[s, :, lane(h)] = dot(flip, query, 1, 0)
+            dvi[s, :, lane(h)] = dot(sct[s, h], d_out, 1, 0)
             attended = factor * (att[s, :, lane(h)] + dot(query, prefix, 1, 0))
             gate = jax.nn.sigmoid(g_v[s, :, lane(h)].astype(F32))
-            d_gate = dgated[:, lane(h)] * attended * gate * (1.0 - gate)
+            d_gate = dgated[s, :, lane(h)] * attended * gate * (1.0 - gate)
             dcat[s, :, lane(1 * heads + h)] = d_gate.astype(BF16)
 
     tile = min(TILE, feat // 2)
@@ -241,8 +241,14 @@
 
         tile_loop(step)
 
-    def part_copy(s, o):
-        return rc(part_send.at[s, o], part_recv.at[s, o], ps.at[s, o], pr.at[s, o], (i, pj))
+    def part_copy(s, o, t):
+        at = pl.ds(pl.multiple_of(t * tile, tile), tile)
+        return rc(
+            part_send.at[s, o, :, at], part_recv.at[s, o, :, at], ps.at[s, o, t], pr.at[s, o, t], (i, pj)
+        )
+
+    def near_copy(s):
+        return rc(part_send.at[s, c], part_recv.at[s, c], ps.at[s, c, 0], pr.at[s, c, 0], (i, pj))
 
     def y_copy(s, d, t):
         o = others[d - 1]
@@ -253,12 +259,14 @@
             ys.at[s, d - 1, t], yr.at[s, to, t], (i, 2 * o + p),
         )
 
-    def for_partner(s, o, whole=False):
-        def put(to, new):
-            part_send[s, o, :, to] = new.astype(BF16)
-
-        tiles(s, 2 * o + 1 - p, put, whole)
-        part_copy(s, o).start()
+    def for_partner(s, o):
+        def step(t):
+            at = pl.ds(pl.multiple_of((2 * o + 1 - p) * feat + t * tile, tile), tile)
+            to = pl.ds(pl.multiple_of(t * tile, tile), tile)
+            part_send[s, o, :, to] = (product(s, at, 2, 4) + acc[:, at]).astype(BF16)
+            part_copy(s, o, t).start()
+
+        tile_loop(step)
 
     def far_begin(s):
         gather_state(qa, s)
@@ -274,9 +282,8 @@
     def far_end(s):
         for d in range(1, chips):
             o = others[d - 1]
-            part_copy(s, o).wait_recv()
-
             def step(t):
+                part_copy(s, o, t).wait_recv()
                 at = pl.ds(pl.multiple_of((2 * o + p) * feat + t * tile, tile), tile)
                 to = pl.ds(pl.multiple_of(t * tile, tile), tile)
                 new = product(s, at, 2, 4) + acc[:, at] + part_recv[s, o, :, to].astype(F32)
@@ -286,20 +293,30 @@
             tile_loop(step)
 
     def near_stage(s, whole):
-        for_partner(s, c, whole)
+        def put(to, new):
+            part_send[s, c, :, to] = new.astype(BF16)
+
+        tiles(s, pj, put, whole)
+        near_copy(s).start()
 
         def put(to, new):
             own[s, :, to] = new
 
-        tiles(s, j, put, whole)
+        tiles(s, j, put, True)
 
     def own_copy(s):
         return pltpu.make_async_copy(own_b.at[s], own_h.at[s], ow.at[s])
 
     def finish(s):
-        part_copy(s, c).wait_recv()
+        near_copy(s).wait_recv()
         own_b[s] = (own[s] + part_recv[s, c].astype(F32)).astype(BF16)
         own_copy(s).start()
+
+    for s in range(seqs):
+        own_loads[s].wait()
+        gated(s, j, True)
+        ag_wait(s, pj)
+        gated(s, pj)
 
     def nothing():
         return None
@@ -309,7 +326,10 @@
     relay_z(ka, 1)
     for load in loads[5:]:
         load.wait()
-    lax.fori_loop(0, n, lambda x, carry: (early(0, x), carry)[1], 0)
+    for o in others:
+        early(0, 2 * o + 1 - p)
+        early(0, 2 * o + p)
+    early(0, pj)
     gate_stage(1, lambda: relay_z(qa, 0), lambda: far_begin(0), nothing)
     far_end(0)
     relay_p(qa, 1)
@@ -335,8 +355,9 @@
         end_state(ka, s)
         end_state(qa, s)
         for o in others:
-            part_copy(s, o).wait_send()
-        part_copy(s, c).wait_send()
+            for t in range(feat // tile):
+                part_copy(s, o, t).wait_send()
+        near_copy(s).wait_send()
         own_copy(s).wait()
         for d in range(1, chips):
             for t in range(feat // tile):
@@ -363,7 +384,7 @@
         vm(tok, BF16), vm(tok, BF16), vm(tok, BF16), vm(tok, BF16),
         vm(w_out.shape, BF16), vm((width, 4 * cols), BF16),
         vm((seqs, n, span, feat), BF16),
-        vm((seqs, heads, span, span), BF16), vm(tok, F32), vm((span, cols), F32),
+        vm((seqs, heads, span, span), BF16), vm((seqs, heads, HD, span), BF16), vm(tok, F32), vm(tok, F32),
         vm(tok, BF16), vm((seqs, span, 4 * cols), BF16), vm(tok, F32), vm(tok, F32), vm((span, width), F32),
         vm(st, BF16), vm(st, BF16), vm(one, BF16), vm(slots, BF16), vm(st, BF16),
         vm(st, BF16), vm(st, BF16), vm(one, BF16), vm(slots, BF16), vm(st, BF16),
@@ -373,7 +394,7 @@
         dma((9,)), dma((seqs,)), dma((seqs, chips)), dma((seqs, chips)), dma((seqs, n)),
         dma((2, seqs, 2)), dma((seqs, groups)), dma((seqs, groups)), dma((2, seqs)),
         dma((2, seqs, 2)), dma((seqs, groups)), dma((seqs, groups)), dma((2, seqs)),
-        dma((seqs, chips)), dma((seqs, chips)), dma((seqs, chips, 2)), dma((seqs, chips, 2)), dma((seqs,)),
+        dma((seqs, chips, 2)), dma((seqs, chips, 2)), dma((seqs, chips, 2)), dma((seqs, chips, 2)), dma((seqs,)),
     ]
     flops = 2 * seqs * span * cols * width * 5
     own, far = pl.pallas_call(

time: 67.3 us -> 66 us (0.981)
  Pallas kernels: 63.6 us -> 62.9 us
where the time goes in v4:
time: 66 us; the launch traced here: 65.8 us
  Pallas kernels  62.9 us (95%)
  other arithmetic  2.92 us (4%)
    pallas_call x1, Pallas kernels, body(): pl.pallas_call(functools.partial(kernel, n, ns), out_shape=(jax.ShapeDtyp...  62.9 us
    convert_element_type x1, other arithmetic, body(): return total.astype(BF16)  2.92 us

profile of v4, /device:TPU:0, one launch (start us, length us, event | category | flops | bytes accessed | tf_op | source)
XLA Modules:
  0.0 65.8 jit_solution(12750985339014159096)
XLA Ops:
  0.0 62.9 %shard_map.100 = (bf16[2,256,1024]{2,1,0:T(8,128)(2,1)}, bf16[1,2,256,1024]{3,2,1,0:T(8,128)(2,1)}) custom-call(bf16[2,256,512]{2,1,0:T(8,128)(2,1)} %q_h.1, bf16[2,256,512]{2,1,0:T(8,128)(2,1)} %k_h.1, bf16[2,256,512]{2,1,0:T(8,128)(2,1)} %v_h.1, bf16[2,256,512]{2,1,0:T(8,128)(2,1)} %g_h.1, bf16[2,256,1024]{2,1,0:T(8,128)(2,1)} %go_h.1, ...), custom_call_target="tpu_custom_call" | custom-call | flops 10737418240 | bytes 20971520 | tf_op jit(solution)/shard_map/pallas_call | solution.py:400
  62.9 2.9 %fusion = bf16[2,256,1024]{2,1,0:T(8,128)(2,1)} fusion(bf16[2,256,1024]{2,1,0:T(8,128)(2,1)} %get-tuple-element.7, bf16[1,2,256,1024]{3,2,1,0:T(8,128)(2,1)} %get-tuple-element.8), kind=kLoop, calls=%fused_computation.1 | loop fusion | flops 2097152 | bytes 3145728 | tf_op jit(solution)/shard_map/convert_element_type | solution.py:417

commit v5 on v4

--- a/solution.py
+++ b/solution.py
@@ -20,7 +20,7 @@
 def kernel(
     n, ns,
     q_h, k_h, v_h, g_h, go_h, wq_h, wk_h, wv_h, wg_h, wo_h, own_h, y_h,
-    q_v, k_v, v_v, g_v, wo_v, w_v, gbuf, sct, q_t, att, dgated, dout, dcat, dki, dvi, acc,
+    q_v, k_v, v_v, g_v, wo_v, w_v, gbuf, sct, q_t, att, dgated, opened, dout, dcat, dki, dvi, acc,
     ks_send, ks_pair, ks_sum, ks_slots, ks_z, qs_send, qs_pair, qs_sum, qs_slots, qs_z, state,
     part_send, part_recv, y_send, own, own_b,
     ld, ld_own, ag_s, ag_f, ag_r, kp, kg_s, kg_r, kz, qp, qg_s, qg_r, qz, ps, pr, ys, yr, ow,
@@ -174,6 +174,7 @@
                 copy.wait_send()
             for copy in far[s + 1]:
                 copy.start()
+        opened[s] = jax.nn.sigmoid(g_v[s].astype(F32))
         before()
         for x, o in enumerate(others):
             src = 2 * o + p
@@ -188,7 +189,7 @@
             ag_wait(s, src)
             gated(s, src)
         for h in range(heads):
-            gate = jax.nn.sigmoid(g_v[s, :, lane(h)].astype(F32))
+            gate = opened[s, :, lane(h)]
             d_out = (dgated[s, :, lane(h)] * gate).astype(BF16)
             dout[s, :, lane(h)] = d_out
             qs_send[s, h // hs, h % hs] = dot(q_t[s, h], d_out, 1, 0).astype(BF16)
@@ -209,7 +210,7 @@
             dki[s, :, lane(h)] = dot(flip, query, 1, 0)
             dvi[s, :, lane(h)] = dot(sct[s, h], d_out, 1, 0)
             attended = factor * (att[s, :, lane(h)] + dot(query, prefix, 1, 0))
-            gate = jax.nn.sigmoid(g_v[s, :, lane(h)].astype(F32))
+            gate = opened[s, :, lane(h)]
             d_gate = dgated[s, :, lane(h)] * attended * gate * (1.0 - gate)
             dcat[s, :, lane(1 * heads + h)] = d_gate.astype(BF16)
 
@@ -384,7 +385,7 @@
         vm(tok, BF16), vm(tok, BF16), vm(tok, BF16), vm(tok, BF16),
         vm(w_out.shape, BF16), vm((width, 4 * cols), BF16),
         vm((seqs, n, span, feat), BF16),
-        vm((seqs, heads, span, span), BF16), vm((seqs, heads, HD, span), BF16), vm(tok, F32), vm(tok, F32),
+        vm((seqs, heads, span, span), BF16), vm((seqs, heads, HD, span), BF16), vm(tok, F32), vm(tok, F32), vm(tok, F32),
         vm(tok, BF16), vm((seqs, span, 4 * cols), BF16), vm(tok, F32), vm(tok, F32), vm((span, width), F32),
         vm(st, BF16), vm(st, BF16), vm(one, BF16), vm(slots, BF16), vm(st, BF16),
         vm(st, BF16), vm(st, BF16), vm(one, BF16), vm(slots, BF16), vm(st, BF16),

time: 66 us -> 66 us (level)
  no operation moved by 1% of the time
where the time goes in v5:
time: 66 us; the launch traced here: 65.9 us
  Pallas kernels  63 us (95%)
  other arithmetic  2.92 us (4%)
    pallas_call x1, Pallas kernels, body(): pl.pallas_call(functools.partial(kernel, n, ns), out_shape=(jax.ShapeDtyp...  63 us
    convert_element_type x1, other arithmetic, body(): return total.astype(BF16)  2.92 us

profile of v5, /device:TPU:0, one launch (start us, length us, event | category | flops | bytes accessed | tf_op | source)
XLA Modules:
  0.0 65.9 jit_solution(8050676736130296128)
XLA Ops:
  0.0 63.0 %shard_map.100 = (bf16[2,256,1024]{2,1,0:T(8,128)(2,1)}, bf16[1,2,256,1024]{3,2,1,0:T(8,128)(2,1)}) custom-call(bf16[2,256,512]{2,1,0:T(8,128)(2,1)} %q_h.1, bf16[2,256,512]{2,1,0:T(8,128)(2,1)} %k_h.1, bf16[2,256,512]{2,1,0:T(8,128)(2,1)} %v_h.1, bf16[2,256,512]{2,1,0:T(8,128)(2,1)} %g_h.1, bf16[2,256,1024]{2,1,0:T(8,128)(2,1)} %go_h.1, ...), custom_call_target="tpu_custom_call" | custom-call | flops 10737418240 | bytes 20971520 | tf_op jit(solution)/shard_map/pallas_call | solution.py:401
  63.0 2.9 %fusion = bf16[2,256,1024]{2,1,0:T(8,128)(2,1)} fusion(bf16[2,256,1024]{2,1,0:T(8,128)(2,1)} %get-tuple-element.7, bf16[1,2,256,1024]{3,2,1,0:T(8,128)(2,1)} %get-tuple-element.8), kind=kLoop, calls=%fused_computation.1 | loop fusion | flops 2097152 | bytes 3145728 | tf_op jit(solution)/shard_map/convert_element_type | solution.py:418
